TPU v7x, 1024 devices: a whole 4x8x16 slice. The times are simulated.
1024 devices in a mesh: member: 16 (over x, z_hi), shard: 64 (over y, z_lo, core).
Axes of the slice: x: 4, y: 8, z: 16 (z_hi: 4, z_lo: 4; z = z_hi * 4 + z_lo), core: 2. Of those that a mesh axis runs over, the one named last changes fastest.
Arguments:
- trunk_out: bfloat16 [128, 8192], P('shard', 'member'), may hold values from -6 to 6
- segment_ids: int32 [128], replicated, may hold values from 0 to 7, never falling along the last dimension, each value on 1 to 32 neighbouring positions
- pair_order: int32 [8], replicated, may hold values from 0 to 7, each once
- w_query: bfloat16 [16, 64, 4096, 128], P('member', 'shard'), may hold values from -0.25 to 0.25
- w_key_value: bfloat16 [16, 64, 512, 256], P('member', 'shard'), may hold values from -0.0625 to 0.0625
- w_out: bfloat16 [16, 4096, 8192], P('member', 'shard'), may hold values from -0.09375 to 0.09375
- norm_gain: float32 [16, 8192], P('member'), may hold values from 0.1 to 1.9
- reward_weight: float32 [16, 8192], P('member'), may hold values from -0.0625 to 0.0625
Outputs:
- trunk_grad: float32 [128, 8192], P('member', 'shard')
- rewards: float32 [16, 8], P('member')
Inputs may be any that keep to these rules, and one draw needn't show every extreme that they name: `segment_ids`: segment numbers never fall along the tokens; every sequence 0 to 7 has 1 to 32 tokens, and one has exactly 32. Each sequence appears once; sequence pair_order[2 * i] is preferred to sequence pair_order[2 * i + 1].
All inputs are finite; a program needn't handle non-finite values.
Results may differ from a plain program's by a relative error of at most 0.011.
Values may be sent and summed in bfloat16 or wider, within the bound.
A program may use at most 32 MiB of HBM per device.

v0:
```python
import math

import jax
import jax.numpy as jnp
from jax import lax
from jax.sharding import PartitionSpec as P

HD = 128
SEQS = 8


softcap_limit = 20.0
loss_scale = 256.0
norm_eps = 1e-05


def from_partner(block, axis, stride):
    count = lax.axis_size(axis)
    route = []
    for low in range(count):
        high = low | 1 << stride
        if high != low and high < count:
            route += [(low, high), (high, low)]
    return lax.ppermute(block, axis, route)


def in_order(pieces, dim):
    pieces = jnp.moveaxis(pieces, 0, dim)
    lengths = pieces.shape
    return pieces.reshape(*lengths[:dim], lengths[dim] * lengths[dim + 1], *lengths[dim + 2 :])


def from_everyone(array, axis):
    copies = jnp.broadcast_to(array, (lax.axis_size(axis), *array.shape))
    return lax.all_to_all(copies, axis, split_axis=0, concat_axis=0, tiled=True)


def gathered_copies(array, axis, dim):
    return in_order(from_everyone(array, axis), dim)


def split_up(array, dim, devices):
    lengths = array.shape
    pieces = array.reshape(*lengths[:dim], devices, lengths[dim] // devices, *lengths[dim + 1 :])
    return jnp.moveaxis(pieces, dim, 0)


def sum_at_owner(array, axis, dim):
    devices = lax.axis_size(axis)
    pieces = lax.all_to_all(split_up(array, dim, devices), axis, 0, 0, tiled=True)
    return jnp.sum(pieces, axis=0)


def partner_swap(values, bit_number):
    return from_partner(values, "shard", bit_number)


def group_total(values, bit_list):
    for bit_number in bit_list:
        values = values + partner_swap(values, bit_number)
    return values


def pair_join(own_part, other_part, pair_side, join_axis):
    first_part = jnp.where(pair_side == 0, own_part, other_part)
    second_part = jnp.where(pair_side == 0, other_part, own_part)
    return jnp.concatenate([first_part, second_part], axis=join_axis)


def on_device(
    trunk_out, segment_ids, pair_order, w_query, w_key_value, w_out, norm_gain, reward_weight
):
    n_shard = lax.axis_size("shard")
    query_heads = n_shard // 2
    kv_count = max(1, query_heads // 8)
    group_size = query_heads // kv_count
    shard_index = lax.axis_index("shard")
    pair_side = shard_index % 2
    head_index = shard_index // 2
    block_index = shard_index % (2 * group_size) // 2
    local_rows, local_width = trunk_out.shape
    features = gathered_copies(trunk_out, "member", 1)
    gathered = lax.all_gather(features, "shard", axis=0, tiled=True)
    tok_count, model_width = gathered.shape
    half_width = model_width // 2
    half_rows = tok_count // 2
    half_head = HD // 2
    row_block = half_width // group_size
    scale_factor = 1.0 / math.sqrt(HD)
    group_bits = list(range((2 * group_size).bit_length() - 1))
    query_piece = w_query[0, 0]
    kv_piece = w_key_value[0, 0]
    out_rows = w_out[0]
    gain_vector = norm_gain[0]
    head_weight = reward_weight[0]
    positions = jnp.arange(tok_count)
    own_start = pair_side * half_rows
    own_positions = own_start + jnp.arange(half_rows)
    own_segments = lax.dynamic_slice_in_dim(segment_ids, own_start, half_rows, 0)
    allowed = (own_segments[:, None] == segment_ids[None, :]) & (
        positions[None, :] <= own_positions[:, None]
    )
    member_of = jnp.arange(SEQS)[:, None] == segment_ids[None, :]
    pooling = member_of.astype(jnp.bfloat16)
    lengths = jnp.sum(member_of.astype(jnp.float32), axis=1)
    own_pooling = lax.dynamic_slice_in_dim(pooling, own_start, half_rows, 1)
    half_features = lax.dynamic_slice_in_dim(gathered, pair_side * half_width, half_width, 1)
    query_partial = jnp.dot(half_features, query_piece, preferred_element_type=jnp.float32)
    kept_rows = lax.dynamic_slice_in_dim(query_partial, own_start, half_rows, 0)
    sent_rows = lax.dynamic_slice_in_dim(query_partial, half_rows - own_start, half_rows, 0)
    queries = (kept_rows + partner_swap(sent_rows, 0)).astype(jnp.bfloat16)
    kv_features = lax.dynamic_slice_in_dim(half_features, block_index * row_block, row_block, 1)
    kv_values = group_total(
        jnp.dot(kv_features, kv_piece, preferred_element_type=jnp.float32), group_bits
    ).astype(jnp.bfloat16)
    key_full = kv_values[:, :HD]
    value_full = kv_values[:, HD:]
    raw_scores = (
        jnp.einsum("td,sd->ts", queries, key_full, preferred_element_type=jnp.float32)
        * scale_factor
    )
    capped = softcap_limit * jnp.tanh(raw_scores / softcap_limit)
    weights_exp = jnp.where(allowed, jnp.exp(capped), 0.0)
    attention = weights_exp / jnp.sum(weights_exp, axis=1, keepdims=True)
    attention_low = attention.astype(jnp.bfloat16)
    attended = jnp.dot(attention_low, value_full, preferred_element_type=jnp.float32).astype(
        jnp.bfloat16
    )
    seq_part = jnp.dot(own_pooling, attended, preferred_element_type=jnp.float32)
    seq_total = seq_part + partner_swap(seq_part, 0)
    seq_mean = (seq_total / lengths[:, None]).astype(jnp.bfloat16)
    own_dims = lax.dynamic_slice_in_dim(seq_mean, pair_side * half_head, half_head, 1)
    head_part = jnp.dot(own_dims, out_rows, preferred_element_type=jnp.float32)
    pooled_attn = lax.psum(head_part, "shard")
    pooled_input = jnp.dot(pooling, gathered, preferred_element_type=jnp.float32) / lengths[:, None]
    hidden = pooled_input + pooled_attn
    inverse_rms = lax.rsqrt(jnp.mean(hidden * hidden, axis=1) + norm_eps)
    normed = hidden * inverse_rms[:, None] * gain_vector
    rewards = jnp.sum(normed * head_weight, axis=1)
    seq_ids = jnp.arange(SEQS)
    chosen = (pair_order[0::2][:, None] == seq_ids[None, :]).astype(jnp.float32)
    rejected = (pair_order[1::2][:, None] == seq_ids[None, :]).astype(jnp.float32)
    margin = jnp.sum(chosen * rewards, axis=1) - jnp.sum(rejected * rewards, axis=1)
    pair_slope = loss_scale * jax.nn.sigmoid(-margin)
    reward_grad = jnp.sum(rejected * pair_slope[:, None], axis=0) - jnp.sum(
        chosen * pair_slope[:, None], axis=0
    )
    scaled_grad = reward_grad[:, None] * head_weight * gain_vector
    hidden_grad = inverse_rms[:, None] * (
        scaled_grad
        - hidden * (inverse_rms**2)[:, None] * jnp.mean(hidden * scaled_grad, axis=1, keepdims=True)
    )
    per_token = hidden_grad / lengths[:, None]
    grad_low = hidden_grad.astype(jnp.bfloat16)
    grad_dims = (
        jnp.einsum("jd,ed->je", grad_low, out_rows, preferred_element_type=jnp.float32)
        / lengths[:, None]
    )
    mean_grad = pair_join(grad_dims, partner_swap(grad_dims, 0), pair_side, 1)
    out_grad = jnp.take(mean_grad, own_segments, axis=0).astype(jnp.bfloat16)
    prob_grad = jnp.einsum("td,sd->ts", out_grad, value_full, preferred_element_type=jnp.float32)
    score_grad = attention * (prob_grad - jnp.sum(attention * prob_grad, axis=1, keepdims=True))
    raw_grad = (score_grad * (1.0 - (capped / softcap_limit) ** 2) * scale_factor).astype(
        jnp.bfloat16
    )
    query_grad = jnp.dot(raw_grad, key_full, preferred_element_type=jnp.float32).astype(
        jnp.bfloat16
    )
    key_grad = jnp.einsum("ts,td->sd", raw_grad, queries, preferred_element_type=jnp.float32)
    value_grad = jnp.einsum(
        "ts,td->sd", attention_low, out_grad, preferred_element_type=jnp.float32
    )
    kv_grad = group_total(jnp.concatenate([key_grad, value_grad], axis=1), group_bits).astype(
        jnp.bfloat16
    )
    query_wire = lax.optimization_barrier(query_grad).astype(jnp.float32)
    query_all = pair_join(
        query_grad, partner_swap(query_wire, 0).astype(jnp.bfloat16), pair_side, 0
    )
    grad_half = jnp.einsum("td,rd->tr", query_all, query_piece, preferred_element_type=jnp.float32)
    kv_term = jnp.einsum("te,re->tr", kv_grad, kv_piece, preferred_element_type=jnp.float32)
    start_col = block_index * row_block
    grad_half = lax.dynamic_update_slice_in_dim(
        grad_half,
        lax.dynamic_slice_in_dim(grad_half, start_col, row_block, 1) + kv_term,
        start_col,
        1,
    )
    pair_rows = 2 * local_rows
    start_row = head_index * pair_rows
    pair_segments = lax.dynamic_slice_in_dim(segment_ids, start_row, pair_rows, 0)
    token_half = lax.dynamic_slice_in_dim(per_token, pair_side * half_width, half_width, 1)
    direct = jnp.take(token_half, pair_segments, axis=0)
    grad_half = lax.dynamic_update_slice_in_dim(
        grad_half,
        lax.dynamic_slice_in_dim(grad_half, start_row, pair_rows, 0) + direct,
        start_row,
        0,
    )
    by_member = lax.psum_scatter(grad_half, "member", scatter_dimension=0, tiled=True)
    member_rows = by_member.shape[0]
    placed = lax.dynamic_update_slice_in_dim(
        jnp.zeros((member_rows, model_width), jnp.float32), by_member, pair_side * half_width, 1
    )
    trunk_grad = sum_at_owner(placed, "shard", 1)
    return (trunk_grad, rewards[None])


def solution(mesh):
    placed = (
        P("shard", "member"),
        P(),
        P(),
        P("member", "shard", None, None),
        P("member", "shard", None, None),
        P("member", "shard", None),
        P("member", None),
        P("member", None),
    )
    return jax.shard_map(
        on_device,
        mesh=mesh,
        in_specs=placed,
        out_specs=(P("member", "shard"), P("member", None)),
        check_vma=False,
    )
```

profile of v0, /device:TPU:1, one launch (start us, length us, event | category | flops | bytes accessed | tf_op | source)
XLA Modules:
  0.0 904.0 jit_solution(4128205695783164129)
XLA Ops:
  8.0 35.7 %all_to_all.10 = bf16[16,2,512]{2,1,0:T(2,128)(2,1)} all-to-all(bf16[16,2,512]{2,1,0:T(2,128)(2,1)S(1)} %broadcast_in_dim.29), channel_id=1, replica_groups=mesh['member'=16,'shard'=64] {'member'}, dimensions={0} | all-to-all | bytes 65536 | tf_op jit(solution)/shard_map/all_to_all | solution.py:35
  43.9 117.3 %all-gather.3.cloned.1.call-done = bf16[64,2,8192]{2,1,0:T(2,128)(2,1)} async-done(((bf16[1,2,8192]{2,1,0:T(2,128)(2,1)}), bf16[64,2,8192]{2,1,0:T(2,128)(2,1)}) %all-gather.3.cloned.1.call-update) | async-done | bytes 2097168 | tf_op jit(solution)/shard_map/all_gather | solution.py:83
  161.2 2.7 reshape.79
  164.2 2.2 collective-permute-start.1
  168.5 2.1 collective-permute-start.2
  171.1 4.2 collective-permute-done.2
  175.3 3.2 collective-permute-start.3
  178.5 3.3 collective-permute-start
  181.8 4.3 collective-permute-done.3
  186.2 1.9 collective-permute-start.4
  188.2 4.5 collective-permute-done.4
  194.6 3.3 collective-permute-start.5
  200.0 2.2 fusion.5
  208.7 498.3 %all-reduce.2.cloned.1.call-done = f32[8,8192]{1,0:T(8,128)} async-done(((f32[8,8192]{1,0:T(8,128)}), f32[8,8192]{1,0:T(8,128)}) %all-reduce.2.cloned.1.call-update) | async-done | bytes 262160 | tf_op jit(solution)/shard_map/psum | solution.py:134
  710.9 4.0 collective-permute-start.6
  717.5 2.2 collective-permute-start.8
  719.9 2.1 collective-permute-start.7
  725.3 3.4 collective-permute-done.9
  728.6 1.9 collective-permute-start.10
  730.6 9.0 collective-permute-done.10
  739.6 1.9 collective-permute-start.11
  742.0 4.0 collective-permute-done.11
  747.7 125.7 %reduce-scatter.2.cloned.1.call-done = f32[8,4096]{1,0:T(8,128)} async-done(((f32[128,4096]{1,0:T(8,128)}), f32[8,4096]{1,0:T(8,128)}) %reduce-scatter.2.cloned.1.call-update) | async-done | bytes 131088 | tf_op jit(solution)/shard_map/reduce_scatter | solution.py:200
  874.4 22.4 %all_to_all.11 = f32[64,8,128]{2,1,0:T(8,128)S(1)} all-to-all(f32[64,8,128]{2,1,0:T(8,128)S(1)} %bitcast.29), channel_id=1, replica_groups=mesh['member'=16,'shard'=64] {'shard'}, dimensions={0} | all-to-all | bytes 524288 | tf_op jit(solution)/shard_map/all_to_all | solution.py:50
  (113 shorter events, 27.6 us)
Async XLA Ops:
  7.2 163.5 %copy-start = (bf16[1,1,4096,128]{3,2,1,0:T(8,128)(2,1)S(1)}, bf16[1,1,4096,128]{3,2,1,0:T(8,128)(2,1)}, u32[]{:S(2)}) copy-start(bf16[1,1,4096,128]{3,2,1,0:T(8,128)(2,1)} %param.11) | copy-start | bytes 3145732
  7.2 154.0 %all-gather.3.cloned.1.call-start = ((), (), s32[]{:S(2)}) async-start(), calls=%async_computation.5 | async-start | bytes 2129920 | tf_op jit(solution)/shard_map/all_gather | solution.py:83
  43.7 663.3 %all-reduce.2.cloned.1.call-start = ((), (), s32[]{:S(2)}) async-start(), calls=%async_computation.3 | async-start | bytes 524288 | tf_op jit(solution)/shard_map/psum | solution.py:134
  43.8 120.1 %copy-start.3 = (bf16[1,1,512,256]{3,2,1,0:T(8,128)(2,1)S(1)}, bf16[1,1,512,256]{3,2,1,0:T(8,128)(2,1)}, u32[]{:S(2)}) copy-start(bf16[1,1,512,256]{3,2,1,0:T(8,128)(2,1)} %param.12) | copy-start | bytes 786436
  43.9 122.5 %copy-start.8 = (s32[128]{0:T(128)S(1)}, s32[128]{0:T(128)}, u32[]{:S(2)}) copy-start(s32[128]{0:T(128)} %param.9) | copy-start | bytes 1540
  164.2 3.4 collective-permute-start.1
  167.6 26.0 %copy-start.11 = (s32[64]{0:T(128)}, s32[64]{0:T(128)S(1)}, u32[]{:S(2)}) copy-start(s32[64]{0:T(128)S(1)} %get-tuple-element.9) | copy-start | bytes 772
  168.5 25.1 %copy-start.22 = (pred[8,128]{1,0:T(8,128)(4,1)S(1)}, pred[8,128]{1,0:T(8,128)(4,1)}, u32[]{:S(2)}) copy-start(pred[8,128]{1,0:T(8,128)(4,1)} %iota_compare_fusion.1) | copy-start | bytes 3076
  168.5 6.7 collective-permute-start.2
  175.3 10.9 %collective-permute-start.3 = (f32[128,256]{1,0:T(8,128)S(1)}, f32[128,256]{1,0:T(8,128)S(1)}, u32[]{:S(2)}, u32[]{:S(2)}) collective-permute-start(f32[128,256]{1,0:T(8,128)S(1)} %add.128), channel_id=1, source_target_pairs={{0,4},{4,0},{1,5},{5,1},{2,6},{6,2},{3,7},{7,3},{8,12},{12,8},{9,1... | collective-permute-start | bytes 393224 | tf_op jit(solution)/shard_map/ppermute | solution.py:24
  178.5 9.6 %collective-permute-start = (f32[64,128]{1,0:T(8,128)S(1)}, f32[64,128]{1,0:T(8,128)S(1)}, u32[]{:S(2)}, u32[]{:S(2)}) collective-permute-start(f32[64,128]{1,0:T(8,128)S(1)} %constant_dynamic-slice_fusion.1), channel_id=1, source_target_pairs={{0,1},{1,0},{2,3},{3,2},{4,5},{5,4},{6,7},{7,6},{8,9},{9,8},{10,11... | collective-permute-start | bytes 98312 | tf_op jit(solution)/shard_map/ppermute | solution.py:24
  181.8 11.8 %copy-start.17 = (s32[64]{0:T(128)}, s32[64]{0:T(128)S(1)}, u32[]{:S(2)}) copy-start(s32[64]{0:T(128)S(1)} %iota_add_fusion) | copy-start | bytes 772
  186.2 6.4 collective-permute-start.4
  194.6 4.6 collective-permute-start.5
  200.0 508.6 %copy-start.4 = (f32[1,8192]{1,0:T(1,128)S(1)}, f32[1,8192]{1,0:T(1,128)}, u32[]{:S(2)}) copy-start(f32[1,8192]{1,0:T(1,128)} %param.15) | copy-start | bytes 98308
  200.0 508.6 %copy-start.5 = (f32[1,8192]{1,0:T(1,128)S(1)}, f32[1,8192]{1,0:T(1,128)}, u32[]{:S(2)}) copy-start(f32[1,8192]{1,0:T(1,128)} %param.14) | copy-start | bytes 98308
  202.3 671.2 %reduce-scatter.2.cloned.1.call-start = ((), (), s32[]{:S(2)}) async-start(), calls=%async_computation.4 | async-start | bytes 2228224 | tf_op jit(solution)/shard_map/reduce_scatter | solution.py:200
  708.6 7.9 copy-start.7
  710.9 4.8 collective-permute-start.6
  717.5 4.5 collective-permute-start.8
  719.9 10.7 %collective-permute-start.7 = (bf16[64,128]{1,0:T(8,128)(2,1)S(1)}, bf16[64,128]{1,0:T(8,128)(2,1)S(1)}, u32[]{:S(2)}, u32[]{:S(2)}) collective-permute-start(bf16[64,128]{1,0:T(8,128)(2,1)S(1)} %convolution_convert_fusion), channel_id=1, source_target_pairs={{0,1},{1,0},{2,3},{3,2},{4,5},{5,4},{6,7},{7,6},{8,9},{9,8},{10,11... | collective-permute-start | bytes 49160 | tf_op jit(solution)/shard_map/ppermute | solution.py:24
  722.0 6.6 collective-permute-start.9
  728.6 11.0 %collective-permute-start.10 = (f32[128,256]{0,1:T(8,128)S(1)}, f32[128,256]{0,1:T(8,128)S(1)}, u32[]{:S(2)}, u32[]{:S(2)}) collective-permute-start(f32[128,256]{0,1:T(8,128)S(1)} %add.138), channel_id=1, source_target_pairs={{0,4},{4,0},{1,5},{5,1},{2,6},{6,2},{3,7},{7,3},{8,12},{12,8},{9,1... | collective-permute-start | bytes 393224 | tf_op jit(solution)/shard_map/ppermute | solution.py:24
  739.6 6.4 collective-permute-start.11
  (14 other events, 72.1 us)
Sparse Core Ops, SparseCore 0:
  43.9 117.2 all-gather.2
  202.4 504.5 all-reduce.1
  747.9 125.5 reduce-scatter.1
where the time goes:
time: 905 us; the launch traced here: 904 us
  waiting for transfers between devices  772 us (85%)
  blocking collectives  58.1 us (6%)
  starting transfers between devices  30.2 us (3%)
  between operations  14.4 us (2%)
  other arithmetic  10.8 us (1%)
  local copies, waits for them, and re-layouts  9.94 us (1%)
    psum x1, waiting for transfers between devices, on_device(): pooled_attn = lax.psum(head_part, 'shard')  498 us
    reduce_scatter x1, waiting for transfers between devices, on_device(): lax.psum_scatter(grad_half, 'member', scatter_dimension=0, tiled=True)  126 us
    all_gather x1, waiting for transfers between devices, on_device(): gathered = lax.all_gather(features, 'shard', axis=0, tiled=True)  117 us
    all_to_all x1, blocking collectives, from_everyone(): return lax.all_to_all(copies, axis, split_axis=0, concat_axis=0, tiled=True)  35.7 us
    ppermute x12, waiting for transfers between devices, from_partner(): return lax.ppermute(block, axis, route)  30.2 us
    ppermute x12, starting transfers between devices, from_partner(): return lax.ppermute(block, axis, route)  30.1 us
    all_to_all x1, blocking collectives, sum_at_owner(): lax.all_to_all(split_up(array, dim, devices), axis, 0, 0, tiled=True)  22.4 us
  transfers between devices with their start and end apart: 15, of which 10 were waited for; matrix products, arithmetic and copies ran while one was open for 1% of the time, Pallas kernels for 0%

commit v1 on v0

v1 whole, which is shorter than its diff:
```python
import functools
import math
import types

import jax
import jax.numpy as jnp
from jax import lax
from jax.experimental import pallas as pl
from jax.experimental.pallas import tpu as pltpu
from jax.sharding import PartitionSpec as P

MESH = pl.DeviceIdType.MESH
F32 = jnp.float32
BF16 = jnp.bfloat16
SEQS = 8
CAP = 20.0
LOSS_SCALE = 256.0
EPS = 1e-05
ZL = 4


def loop(count, body):
    def step(index, carry):
        body(index)
        return carry

    lax.fori_loop(0, count, step, 0)


def matmul(a, b, contract=((1,), (0,))):
    return lax.dot_general(a, b, (contract, ((), ())), preferred_element_type=F32)


def scratch_list(dims):
    X, ZH, Y = dims
    tok = 16 * Y
    owned = tok // 16
    heads = 4 * Y
    blocks = heads // 4
    rows = 8 * ZH
    dma = pltpu.SemaphoreType.DMA
    return dict(
        wq=pltpu.VMEM((heads * 128, 128), BF16),
        wkv=pltpu.VMEM((heads * 16, 256), BF16),
        wo=pltpu.VMEM((64, heads * 256), BF16),
        gain=pltpu.VMEM((1, heads * 256), F32),
        weight=pltpu.VMEM((1, heads * 256), F32),
        pair_out=pltpu.VMEM((8, 128), F32),
        pair_in=pltpu.VMEM((8, 128), F32),
        z_out=pltpu.VMEM((8, 128), F32),
        z_in=pltpu.VMEM((ZH * ZL, 8, 128), F32),
        own=pltpu.VMEM((ZH, Y, 2, 16, 128), BF16),
        feat=pltpu.VMEM((X, ZH, Y, 2, 16, 128), BF16),
        q_out=pltpu.VMEM((tok, 128), F32),
        q_in=pltpu.VMEM((tok, 128), F32),
        kv_out=pltpu.VMEM((16, 2, owned, 128), F32),
        kv_in=pltpu.VMEM((16, 2, owned, 128), F32),
        kv_all=pltpu.VMEM((16, 2 * owned, 128), BF16),
        head_out=pltpu.VMEM((heads, 8, 128), F32),
        head_in=pltpu.VMEM((heads, 8, 128), F32),
        part_out=pltpu.VMEM((heads, 8, 128), F32),
        part_in=pltpu.VMEM((heads, 8, 128), F32),
        half=pltpu.VMEM((heads, 8, 128), F32),
        hidden=pltpu.VMEM((2, heads, 8, 128), F32),
        dims_out=pltpu.VMEM((8, 128), F32),
        dims_in=pltpu.VMEM((8, 128), F32),
        dkv_out=pltpu.VMEM((16, 2, owned, 128), F32),
        dkv_in=pltpu.VMEM((8, 2, owned, 128), F32),
        dkv_all=pltpu.VMEM((16, 2 * owned, 128), BF16),
        token_out=pltpu.VMEM((2 * heads, 8, 128), F32),
        term=pltpu.VMEM((4, tok, 128), F32),
        x_out=pltpu.VMEM((blocks, X, 2, 2, rows, 128), BF16),
        x_in=pltpu.VMEM((blocks, X, 2, 2, rows, 128), BF16),
        y_out=pltpu.VMEM((blocks, 2, 2, rows, 128), BF16),
        y_in=pltpu.VMEM((Y, ZL, rows, 128), BF16),
        l_out=pltpu.VMEM((ZL * ZH, 8, 128), F32),
        l_in=pltpu.VMEM((ZL * ZH, 8, 128), F32),
        w_sem=dma((5,)),
        pair_s=dma,
        pair_r=dma,
        z_s=dma,
        z_r=dma((ZH,)),
        ya_s=dma,
        ya_r=dma((ZH,)),
        xa_s=dma,
        xa_s0=dma,
        xa_r=dma((X, ZH)),
        q_s=dma,
        q_r=dma,
        kv_s=dma,
        kv_r=dma,
        kva_s=dma,
        kva_r=dma,
        h1_s=dma,
        h1_r=dma,
        h2_s=dma,
        h2_r=dma,
        h3_s=dma,
        h3_r=dma,
        h4_s=dma,
        h4_r=dma,
        d_s=dma,
        d_r=dma,
        dkv_s=dma,
        dkv_r=dma,
        dka_s=dma,
        dka_r=dma,
        ex_s=dma((blocks,)),
        ex_r=dma((blocks,)),
        ey_s=dma((blocks, 2)),
        ey_r=dma((Y,)),
        el_s=dma,
        el_r=dma,
    )


def kernel(
    dims, names, trunk_ref, seg_ref, order_ref, wq_hbm, wkv_hbm, wo_hbm, gain_hbm, weight_hbm, out_ref, reward_ref, *scratch
):
    r = types.SimpleNamespace(**dict(zip(names, scratch)))
    pending = []
    X, ZH, Y = dims
    XH = X // 2
    tok = 16 * Y
    owned = tok // 16
    heads = 4 * Y
    tiles = 2 * heads
    blocks = heads // 4
    rows = 8 * ZH
    kv_tiles = heads // 8
    scale = 1.0 / math.sqrt(128)

    member = lax.axis_index("member")
    shard = lax.axis_index("shard")
    x, zh = member // ZH, member % ZH
    y, zl, c = shard // (2 * ZL), shard % (2 * ZL) // 2, shard % 2
    p = c * ZL + zl
    ybit = y % 2
    group_y = y - ybit
    o = ybit * 8 + p
    block = ybit * ZL + zl
    head = y * ZL + zl
    xs = x % XH
    target_core = x // XH

    def at(x_=x, zh_=zh, y_=y, zl_=zl, c_=c):
        return (x_ * ZH + zh_, (y_ * ZL + zl_) * 2 + c_)

    def send(src, dst, send_sem, recv_sem, device):
        pltpu.make_async_remote_copy(
            src_ref=src, dst_ref=dst, send_sem=send_sem, recv_sem=recv_sem, device_id=device, device_id_type=MESH
        ).start()

    def wait(sem, ref):
        pltpu.make_async_copy(ref, ref, sem).wait()

    def later(sem, ref):
        pending.append(lambda: wait(sem, ref))

    def z_peer(index):
        other = (zh * ZL + zl + 1 + index) % (ZH * ZL)
        return other, at(zh_=other // ZL, zl_=other % ZL)

    def head_peer(index):
        other = (head + 1 + index) % heads
        return other, at(y_=other // ZL, zl_=other % ZL)

    def group_peer(index):
        other = (o + 1 + index) % 16
        q = other % 8
        return other, at(y_=group_y + other // 8, zl_=q % ZL, c_=q // ZL)

    weight_copies = [
        pltpu.make_async_copy(wq_hbm, r.wq, r.w_sem.at[0]),
        pltpu.make_async_copy(wkv_hbm, r.wkv, r.w_sem.at[1]),
        pltpu.make_async_copy(wo_hbm, r.wo, r.w_sem.at[2]),
        pltpu.make_async_copy(gain_hbm, r.gain, r.w_sem.at[3]),
        pltpu.make_async_copy(weight_hbm, r.weight, r.w_sem.at[4]),
    ]
    for copy in weight_copies:
        copy.start()

    barrier = pltpu.get_barrier_semaphore()

    def greet(device):
        pl.semaphore_signal(barrier, inc=1, device_id=device, device_id_type=MESH)

    loop(ZH * ZL - 1, lambda i: greet(z_peer(i)[1]))
    loop(4 * (Y - 1), lambda i: greet(at(y_=(y + 1 + i // ZL) % Y, zl_=i % ZL)))
    loop(Y - 1, lambda i: greet(at(y_=(y + 1 + i) % Y, c_=1 - c)))
    loop(6, lambda i: greet(at(y_=group_y + i // 3, zl_=(zl + 1 + i % 3) % ZL, c_=1 - c)))
    loop(2 * (X - 1), lambda i: greet(at(x_=(x + 1 + i // 2) % X, c_=i % 2)))
    greet(at(c_=1 - c))
    for k in range(4):
        r.pair_out[2 * k : 2 * k + 2] = trunk_ref[:, k * 128 : (k + 1) * 128].astype(F32)
    pl.semaphore_wait(barrier, ZH * ZL + 5 * (Y - 1) + 6 + 2 * (X - 1))

    send(r.pair_out, r.pair_in, r.pair_s, r.pair_r, at(c_=1 - c))
    later(r.pair_s, r.pair_in)

    row_id = lax.broadcasted_iota(jnp.int32, (SEQS, tok), 0)
    pooling = (row_id == seg_ref[...]).astype(F32)
    lengths = jnp.sum(pooling, axis=1, keepdims=True)
    pooling = pooling.astype(BF16)
    row = lax.broadcasted_iota(jnp.int32, (32, 32), 0)
    col = lax.broadcasted_iota(jnp.int32, (32, 32), 1)
    place = (((row >> 2) & 3) << 3) + (((row >> 1) & 1) << 2) + ((row >> 4) << 1) + (row & 1)
    pick = (col == place).astype(F32).astype(BF16)

    wait(r.pair_r, r.pair_in)
    first = jnp.where(c == 0, r.pair_out[0:4], r.pair_in[4:8])
    second = jnp.where(c == 0, r.pair_in[0:4], r.pair_out[4:8])
    r.z_out[0:4] = first
    r.z_out[4:8] = second
    z = zh * ZL + zl

    def z_send(i):
        send(r.z_out, r.z_in.at[z], r.z_s, r.z_r.at[zh], z_peer(i)[1])

    loop(ZH * ZL - 1, z_send)
    later(r.z_s, r.z_in.at[0 : ZH * ZL - 1])
    pltpu.make_async_copy(r.z_out, r.z_in.at[z], r.z_r.at[zh]).start()

    kv_first = block * kv_tiles // 4
    kv_low, kv_high = kv_first // ZH, kv_first % ZH
    mine = c * XH + xs

    def turn(i):
        return (kv_high + i) % ZH

    def to_y(i):
        h = turn(i)
        wait(r.z_r.at[h], r.z_in.at[0:ZL])
        rows_in = r.z_in[pl.ds(h * ZL, ZL)].reshape(32, 128).astype(BF16)
        r.own[h, y] = matmul(pick, rows_in).astype(BF16).reshape(2, 16, 128)

        def one(j):
            send(r.own.at[h, y], r.own.at[h, y], r.ya_s, r.ya_r.at[h], at(y_=(y + 1 + j) % Y))

        loop(Y - 1, one)

    loop(ZH, to_y)
    later(r.ya_s, r.own.at[:, 0 : Y - 1])

    def to_x(i):
        h = turn(i)
        wait(r.ya_r.at[h], r.own.at[0, 0 : Y - 1])

        def one(j):
            send(
                r.own.at[h], r.feat.at[mine, h], r.xa_s, r.xa_r.at[mine, h],
                at(x_=(x + 1 + j) % X, c_=target_core),
            )

        loop(X - 1, one)

        @pl.when(c == target_core)
        def _():
            pltpu.make_async_copy(r.own.at[h], r.feat.at[mine, h], r.xa_r.at[mine, h]).start()

        @pl.when(c != target_core)
        def _():
            send(r.own.at[h], r.feat.at[mine, h], r.xa_s0, r.xa_r.at[mine, h], at(c_=target_core))

    loop(ZH, to_x)
    later(r.xa_s, r.feat.at[0 : X - 1])

    def settle_own():
        @pl.when(c != target_core)
        def _():
            wait(r.xa_s0, r.feat.at[0])

    pending.append(settle_own)

    same = matmul(pooling, pooling, ((0,), (0,)))
    below = lax.broadcasted_iota(jnp.int32, (tok, tok), 1) <= lax.broadcasted_iota(jnp.int32, (tok, tok), 0)
    allowed = jnp.where(below, same, 0.0) > 0.5

    def feature_tile(index):
        part = index % 4
        return r.feat[part // 2 * XH + index // (4 * ZH), index // 4 % ZH, :, part % 2].reshape(tok, 128)

    weight_copies[0].wait()
    weight_copies[1].wait()

    def query_step(i, total):
        h = turn(i)
        for src in range(X):
            if i > 0:
                wait(r.xa_r.at[src, h], r.feat.at[src, 0])
            cs, x_low = src // XH, src % XH
            start = pl.multiple_of((x_low * ZH + h) * 512 + cs * 256, 256)
            lhs = jnp.concatenate([r.feat[src, h, :, k].reshape(tok, 128) for k in range(2)], axis=1)
            total = total + matmul(lhs, r.wq[pl.ds(start, 256), :])
        return total

    for src in range(X):
        wait(r.xa_r.at[src, turn(0)], r.feat.at[src, 0])
    kv_part = jnp.zeros((tok, 256), F32)
    for k in range(kv_tiles):
        kv_part = kv_part + matmul(feature_tile(block * kv_tiles + k), r.wkv[k * 128 : (k + 1) * 128, :])
    r.kv_out[:, 0] = kv_part[:, :128].reshape(16, owned, 128)
    r.kv_out[:, 1] = kv_part[:, 128:].reshape(16, owned, 128)

    def kv_send(i):
        other, device = group_peer(i)
        send(r.kv_out.at[other], r.kv_in.at[o], r.kv_s, r.kv_r, device)

    loop(15, kv_send)
    later(r.kv_s, r.kv_in.at[0:15])
    r.kv_in[o] = r.kv_out[o]
    q_part = jnp.zeros((tok, 128), F32)
    for i in range(ZH - 1):
        q_part = query_step(i, q_part)
    wait(r.kv_r, r.kv_in.at[0:15])
    r.kv_all[o] = jnp.sum(r.kv_in[...], axis=0).reshape(2 * owned, 128).astype(BF16)

    def kv_share(i):
        send(r.kv_all.at[o], r.kv_all.at[o], r.kva_s, r.kva_r, group_peer(i)[1])

    loop(15, kv_share)
    later(r.kva_s, r.kv_all.at[0:15])
    r.q_out[...] = query_step(ZH - 1, q_part)
    send(r.q_out, r.q_in, r.q_s, r.q_r, at(c_=1 - c))
    later(r.q_s, r.q_in)

    pooled_in = matmul(pooling, feature_tile(head)) / lengths
    wait(r.q_r, r.q_in)
    queries = (r.q_out[...] + r.q_in[...]).astype(BF16)

    wait(r.kva_r, r.kv_all.at[0:15])
    kv = r.kv_all[...].astype(F32)
    keys = kv[:, :owned].reshape(tok, 128).astype(BF16)
    values = kv[:, owned:].reshape(tok, 128).astype(BF16)

    scores = matmul(queries, keys, ((1,), (1,))) * scale
    bent = jnp.tanh(scores / CAP)
    weights = jnp.where(allowed, jnp.exp(CAP * bent), 0.0)
    attention = weights / jnp.sum(weights, axis=1, keepdims=True)
    attention_low = attention.astype(BF16)
    attended = matmul(attention_low, values).astype(BF16)
    means = (matmul(pooling, attended) / lengths).astype(BF16).astype(F32)
    own_dims = jnp.where(c == 0, means[:, :64], means[:, 64:]).astype(BF16)

    weight_copies[2].wait()

    def project(side, target):
        for q in range(heads // 8):
            start = pl.multiple_of(side * (heads * 128) + q * 1024, 1024)
            piece = matmul(own_dims, r.wo[:, pl.ds(start, 1024)])
            for k in range(8):
                target[q * 8 + k] = piece[:, k * 128 : (k + 1) * 128]

    project(1 - c, r.head_out)
    send(r.head_out, r.head_in, r.h1_s, r.h1_r, at(c_=1 - c))
    later(r.h1_s, r.head_in)
    project(c, r.part_out)
    wait(r.h1_r, r.head_in)
    r.part_out[...] = r.part_out[...] + r.head_in[...]

    def part_send(i):
        other, device = head_peer(i)
        send(r.part_out.at[other], r.part_in.at[head], r.h2_s, r.h2_r, device)

    loop(heads - 1, part_send)
    later(r.h2_s, r.part_in.at[0 : heads - 1])
    r.part_in[head] = r.part_out[head]
    wait(r.h2_r, r.part_in.at[0 : heads - 1])
    r.half[head] = jnp.sum(r.part_in[...], axis=0) + pooled_in

    def half_send(i):
        send(r.half.at[head], r.half.at[head], r.h3_s, r.h3_r, head_peer(i)[1])

    loop(heads - 1, half_send)
    later(r.h3_s, r.half.at[0 : heads - 1])
    wait(r.h3_r, r.half.at[0 : heads - 1])
    send(r.half, r.hidden.at[c], r.h4_s, r.h4_r, at(c_=1 - c))
    later(r.h4_s, r.half)
    r.hidden[c] = r.half[...]
    weight_copies[3].wait()
    weight_copies[4].wait()
    gains = r.gain[...] * r.weight[...]
    wait(r.h4_r, r.half)

    hidden = jnp.concatenate([r.hidden[side, k] for side in range(2) for k in range(heads)], axis=1)
    width = tiles * 128
    squares = jnp.sum(hidden * hidden, axis=1, keepdims=True)
    weighted = jnp.sum(hidden * gains, axis=1, keepdims=True)
    rinv = lax.rsqrt(squares / width + EPS)
    rewards = rinv * weighted
    wide = jnp.broadcast_to(rewards, (SEQS, 128))
    row_id = lax.broadcasted_iota(jnp.int32, (SEQS, 128), 0)
    lane = lax.broadcasted_iota(jnp.int32, (SEQS, 128), 1)
    flat = jnp.sum(jnp.where(row_id == lane, wide, 0.0), axis=0, keepdims=True)
    reward_ref[...] = flat[:, :SEQS]
    partner = jnp.zeros((SEQS, 128), F32)
    sign = jnp.zeros((SEQS, 128), F32)
    for k in range(SEQS // 2):
        chosen, rejected = order_ref[2 * k], order_ref[2 * k + 1]
        is_chosen, is_rejected = row_id == chosen, row_id == rejected
        partner = jnp.where(is_chosen & (lane == rejected) | is_rejected & (lane == chosen), flat, partner)
        sign = jnp.where(is_chosen, -1.0, jnp.where(is_rejected, 1.0, sign))
    partner = jnp.sum(partner, axis=1, keepdims=True)
    sign = sign[:, :1]
    slope = sign * LOSS_SCALE / (1.0 + jnp.exp(sign * (partner - rewards)))
    pooled_grad = rinv * (slope * gains - hidden * (rinv * rinv * slope * weighted / width))
    dims_part = matmul(pooled_grad.astype(BF16), r.wo[...], ((1,), (1,))) / lengths
    r.dims_out[...] = jnp.concatenate([dims_part, dims_part], axis=1)
    send(r.dims_out, r.dims_in, r.d_s, r.d_r, at(c_=1 - c))
    later(r.d_s, r.dims_in)
    per_token = pooled_grad / lengths
    for k in range(tiles):
        r.token_out[k] = per_token[:, k * 128 : (k + 1) * 128]
    direct = r.token_out[c * heads + head]
    high = direct.astype(BF16)
    low = (direct - high.astype(F32)).astype(BF16)
    direct = matmul(pooling, high, ((0,), (0,))) + matmul(pooling, low, ((0,), (0,)))
    wait(r.d_r, r.dims_in)
    mine_first = (lane < 64) == (c == 0)
    mean_grad = jnp.where(mine_first, r.dims_out[...], r.dims_in[...])

    out_grad = matmul(pooling, mean_grad.astype(BF16), ((0,), (0,))).astype(BF16)
    prob_grad = matmul(out_grad, values, ((1,), (1,)))
    score_grad = attention * (prob_grad - jnp.sum(attention * prob_grad, axis=1, keepdims=True))
    raw_grad = (score_grad * (1.0 - bent * bent) * scale).astype(BF16)
    key_grad = matmul(raw_grad, queries, ((0,), (0,)))
    value_grad = matmul(attention_low, out_grad, ((0,), (0,)))
    r.dkv_out[:, 0] = key_grad.reshape(16, owned, 128)
    r.dkv_out[:, 1] = value_grad.reshape(16, owned, 128)
    own_head = ybit * ZL + zl

    def dkv_send(i):
        other = (own_head + 1 + i) % 8
        send(
            r.dkv_out.at[other // ZL * 8 + c * ZL + other % ZL], r.dkv_in.at[own_head], r.dkv_s, r.dkv_r,
            at(y_=group_y + other // ZL, zl_=other % ZL),
        )

    loop(7, dkv_send)
    later(r.dkv_s, r.dkv_in.at[0:7])
    r.dkv_in[own_head] = r.dkv_out[o]
    query_grad = matmul(raw_grad, keys).astype(BF16)

    kv_block = block * kv_tiles // 4

    def x_send(index, extra=False):
        start = pl.multiple_of(index * 512, 512)
        piece = matmul(query_grad, r.wq[pl.ds(start, 512), :], ((1,), (1,)))
        for t in range(4):
            part = piece[:, t * 128 : (t + 1) * 128]
            part = jnp.where(index * 4 + t == head, part + direct, part)
            if extra:
                part = part + r.term[t]
            r.x_out[index, :, t % 2, t // 2] = part.astype(BF16).reshape(X, rows, 128)

        def one(i):
            other = (x + 1 + i) % X
            send(r.x_out.at[index, other], r.x_in.at[index, x], r.ex_s.at[index], r.ex_r.at[index], at(x_=other))

        loop(X - 1, one)

    def y_send(index):
        wait(r.ex_r.at[index], r.x_in.at[index, 0 : X - 1])
        total = r.x_out[index, x].astype(F32)
        for i in range(X - 1):
            total = total + r.x_in[index, (x + 1 + i) % X].astype(F32)
        r.y_out[index] = total.astype(BF16)
        y_to = c * (Y // 2) + index // 2
        place = pl.ds(index % 2 * 2, 2)
        for core in range(2):
            here = (y_to == y) & (c == core)

            @pl.when(here)
            def _():
                pltpu.make_async_copy(r.y_out.at[index, core], r.y_in.at[y, place], r.ey_r.at[y]).start()

            @pl.when(jnp.logical_not(here))
            def _():
                send(
                    r.y_out.at[index, core], r.y_in.at[y, place], r.ey_s.at[index, core], r.ey_r.at[y],
                    at(y_=y_to, c_=core),
                )

    def at_turn(i):
        return (kv_block + 1 + i) % blocks

    loop(blocks - 1, lambda i: x_send(at_turn(i)))

    wait(r.dkv_r, r.dkv_in.at[0:7])
    r.dkv_all[o] = jnp.sum(r.dkv_in[...], axis=0).reshape(2 * owned, 128).astype(BF16)

    def dkv_share(i):
        send(r.dkv_all.at[o], r.dkv_all.at[o], r.dka_s, r.dka_r, group_peer(i)[1])

    loop(15, dkv_share)
    later(r.dka_s, r.dkv_all.at[0:15])
    early = blocks // 2
    loop(early, lambda i: y_send(at_turn(i)))
    wait(r.dka_r, r.dkv_all.at[0:15])
    dkv = r.dkv_all[...].astype(F32)
    dkv = jnp.concatenate([dkv[:, :owned].reshape(tok, 128), dkv[:, owned:].reshape(tok, 128)], axis=1).astype(BF16)
    kv_term = matmul(dkv, r.wkv[...], ((1,), (1,)))
    if kv_tiles < 4:
        r.term[...] = jnp.zeros_like(r.term)
    for k in range(kv_tiles):
        r.term[block * kv_tiles % 4 + k] = kv_term[:, k * 128 : (k + 1) * 128]
    x_send(kv_block, True)
    loop(blocks - early, lambda i: y_send(at_turn(early + i)))

    def settle_block(index):
        wait(r.ex_s.at[index], r.x_in.at[index, 0 : X - 1])
        for core in range(2):

            @pl.when(jnp.logical_not((c * (Y // 2) + index // 2 == y) & (c == core)))
            def _():
                wait(r.ey_s.at[index, core], r.y_out.at[index, core])

    pending.append(lambda: loop(blocks, settle_block))

    def y_wait(i):
        wait(r.ey_r.at[i], r.y_in.at[i])

    loop(Y, y_wait)
    total = r.y_in[0].astype(F32)
    for i in range(1, Y):
        total = total + r.y_in[i].astype(F32)
    for k in range(ZL):
        for h in range(ZH):
            r.l_out[h * ZL + k] = total[k, h * 8 : (h + 1) * 8]

    def l_send(i):
        other, device = z_peer(i)
        send(r.l_out.at[other], r.l_in.at[z], r.el_s, r.el_r, device)

    loop(ZH * ZL - 1, l_send)
    later(r.el_s, r.l_in.at[0 : ZH * ZL - 1])
    r.l_in[z] = r.l_out[z]
    wait(r.el_r, r.l_in.at[0 : ZH * ZL - 1])
    out_ref[...] = jnp.sum(r.l_in[...], axis=0)

    for settle in pending:
        settle()


def on_device(dims, trunk_out, segment_ids, pair_order, w_query, w_key_value, w_out, norm_gain, reward_weight):
    scratch = scratch_list(dims)
    vmem = pl.BlockSpec(memory_space=pltpu.VMEM)
    smem = pl.BlockSpec(memory_space=pltpu.SMEM)
    hbm = pl.BlockSpec(memory_space=pl.ANY)
    return pl.pallas_call(
        functools.partial(kernel, dims, tuple(scratch)),
        out_shape=(jax.ShapeDtypeStruct((8, 128), F32), jax.ShapeDtypeStruct((1, SEQS), F32)),
        in_specs=[vmem, vmem, smem] + [hbm] * 5,
        out_specs=(vmem, vmem),
        scratch_shapes=tuple(scratch.values()),
        compiler_params=pltpu.CompilerParams(
            collective_id=0, has_side_effects=True, vmem_limit_bytes=63 * 1024 * 1024
        ),
    )(
        trunk_out, segment_ids.reshape(1, -1), pair_order, w_query[0, 0], w_key_value[0, 0], w_out[0], norm_gain,
        reward_weight,
    )


def solution(mesh):
    members, shards = mesh.shape["member"], mesh.shape["shard"]
    z_high = 4 if members > 4 else 2
    dims = (members // z_high, z_high, shards // (2 * ZL))
    placed = (
        P("shard", "member"),
        P(),
        P(),
        P("member", "shard", None, None),
        P("member", "shard", None, None),
        P("member", "shard", None),
        P("member", None),
        P("member", None),
    )
    return jax.shard_map(
        functools.partial(on_device, dims),
        mesh=mesh,
        in_specs=placed,
        out_specs=(P("member", "shard"), P("member", None)),
        check_vma=False,
    )
```

time: 905 us -> 102 us (0.11)
  waiting for transfers between devices: 772 us -> 0 us
  Pallas kernels: 0 us -> 99.1 us
  blocking collectives: 58.1 us -> 0 us
  starting transfers between devices: 30.2 us -> 0 us
  between operations: 14.4 us -> 0.65 us
  other arithmetic: 10.8 us -> 0 us
    psum x1 -> x0, waiting for transfers between devices: 498 us -> none  [on_device(): pooled_attn = lax.psum(head_part, 'shard')]
    reduce_scatter x1 -> x0, waiting for transfers between devices: 126 us -> none  [on_device(): lax.psum_scatter(grad_half, 'member', scatter_dimension=0, tiled=True)]
    all_gather x1 -> x0, waiting for transfers between devices: 117 us -> none  [on_device(): gathered = lax.all_gather(features, 'shard', axis=0, tiled=True)]
    pallas_call x0 -> x1, Pallas kernels: none -> 99.1 us  [on_device(): pl.pallas_call(functools.partial(kernel, dims, tuple(scratch)), out_shape...]
    all_to_all x2 -> x0, blocking collectives: 58.1 us -> none  [the longest x1 35.7 us: from_everyone(): return lax.all_to_all(copies, axis, split_axis=0, concat_axis=0, tiled=True)]
    ppermute x12 -> x0, waiting for transfers between devices: 30.2 us -> none  [from_partner(): return lax.ppermute(block, axis, route)]
    ppermute x12 -> x0, starting transfers between devices: 30.1 us -> none  [from_partner(): return lax.ppermute(block, axis, route)]
  transfers between devices with their start and end apart: 15 -> 0, of which waited for: 10 -> 0; matrix products, arithmetic and copies ran while one was open for 1% -> 0% of each run, Pallas kernels for 0% -> 0%
where the time goes in v1:
time: 102 us
  Pallas kernels  99.1 us (97%)
  local copies, waits for them, and re-layouts  1.78 us (2%)
    pallas_call x1, Pallas kernels, on_device(): pl.pallas_call(functools.partial(kernel, dims, tuple(scratch)), out_shape...  99.1 us

profile of v1, /device:TPU:1, one launch (start us, length us, event | category | flops | bytes accessed | tf_op | source)
XLA Modules:
  0.0 101.6 jit_solution(12959732099032110894)
XLA Ops:
  0.6 99.1 %shard_map.95 = (f32[8,128]{1,0:T(8,128)}, f32[1,8]{1,0:T(1,128)}) custom-call(bf16[2,512]{1,0:T(2,128)(2,1)} %trunk_ref.1, s32[1,128]{1,0:T(1,128)} %bitcast.7, s32[8]{0:T(128)} %order_ref.1, bf16[4096,128]{1,0:T(8,128)(2,1)} %bitcast.4, bf16[512,256]{1,0:T(8,128)(2,1)} %bitcast.6, bf16[64,8192]{1,0:T(8,128)(2,1)} %bitcast.5, f32[1,8192]{1,0:T(1,128)} %gain_hbm.1, ...), custom_call_target="tpu_custom_call" | custom-call | tf_op jit(solution)/shard_map/pallas_call | solution.py:550
  99.8 0.0 copy-start
  99.8 1.3 %copy.12 = f32[8,128]{1,0:T(8,128)} copy(f32[8,128]{1,0:T(8,128)} %get-tuple-element.4) | data formatting | bytes 8192
  101.1 0.0 copy-done
  101.1 0.5 copy.13
Async XLA Ops:
  99.8 1.3 %copy-start = (f32[1,8]{1,0:T(1,128)S(1)}, f32[1,8]{1,0:T(1,128)}, u32[]{:S(2)}) copy-start(f32[1,8]{1,0:T(1,128)} %get-tuple-element.5) | copy-start | bytes 100
